TPU v7x, 32 devices: a whole 2x2x4 slice. The times are simulated.
32 devices in a mesh: grp: 1, filt: 32 (over z, y, x, core).
Axes of the slice: x: 2, y: 2, z: 4, core: 2. Of those that a mesh axis runs over, the one named last changes fastest.
Arguments:
- code_maps: bfloat16 [256, 512, 512], P('filt', 'grp'), may hold values from -6 to 6
- dual_maps: bfloat16 [256, 512, 512], P('filt', 'grp'), may hold values from -4 to 4
- survey_tile: float32 [512, 512], P('grp'), may hold values from -192 to 192
- filters: float32 [256, 121], P('filt', 'grp'), may hold values from -6 to 6
- valid_blocks: int32 [4], P('grp'), may hold values from 0 to 1, as said below
Outputs:
- new_codes: bfloat16 [256, 512, 512], P('filt', 'grp')
- new_duals: bfloat16 [256, 512, 512], P('filt', 'grp')
- new_filters: float32 [256, 121], P('filt', 'grp')
Inputs may be any that keep to these rules, and one draw needn't show every extreme that they name: `valid_blocks`: exactly 2 of the 4 blocks are 1, the others 0.
All inputs are finite; a program needn't handle non-finite values.
Results may differ from a plain program's by a relative error of at most 0.012.
The roundings to bfloat16 on the way count: a program that leaves them out, or rounds other values in their place, can miss the bound.
Values sent between devices are 32-bit elements; how exact they have to be, the bound alone decides.
A program may use at most 256 MiB of HBM per device.

v0:
```python
import math

import jax
import jax.numpy as jnp
from jax import lax
from jax.sharding import PartitionSpec as P

FS = 11
MB = 128


penalty = 128.0
shrink_level = 1.0
dict_scale = 0.0625
norm_eps = 1e-06


def dft_tables(tile_side):
    indices = jnp.arange(tile_side, dtype=jnp.int32)
    phases = indices[:, None] * indices[None, :] % tile_side
    angles = phases.astype(jnp.float32) * (2.0 * math.pi / tile_side)
    return (jnp.cos(angles), jnp.sin(angles))


def forward_batch(sources, cos_sin, stacked):
    tile_side = sources.shape[1]
    halves = jnp.einsum("kij,jc->kic", sources, cos_sin, preferred_element_type=jnp.float32).astype(
        jnp.bfloat16
    )
    blocks = jnp.einsum("fi,kic->kfc", stacked, halves, preferred_element_type=jnp.float32)
    real_part = blocks[:, :tile_side, :tile_side] - blocks[:, tile_side:, tile_side:]
    imag_part = -(blocks[:, :tile_side, tile_side:] + blocks[:, tile_side:, :tile_side])
    return (real_part, imag_part)


def inverse_batch(real_part, imag_part, cos_sin, neg_table):
    tile_side = real_part.shape[1]
    stack_in = jnp.concatenate([real_part, imag_part], axis=1)
    blocks = jnp.einsum("kij,jc->kic", stack_in, cos_sin, preferred_element_type=jnp.float32)
    q_real = blocks[:, :tile_side, :tile_side] - blocks[:, tile_side:, tile_side:]
    q_imag = blocks[:, :tile_side, tile_side:] + blocks[:, tile_side:, :tile_side]
    merged = jnp.concatenate([q_real, q_imag], axis=1).astype(jnp.bfloat16)
    return jnp.einsum("fi,kic->kfc", neg_table, merged, preferred_element_type=jnp.float32) / float(
        tile_side * tile_side
    )


def inverse_exact(real_part, imag_part, cos_sin_wide, neg_table):
    tile_side = real_part.shape[0]
    stack_in = jnp.concatenate([real_part, imag_part], axis=0)
    blocks = jnp.dot(
        stack_in, cos_sin_wide, precision=lax.Precision.HIGHEST, preferred_element_type=jnp.float32
    )
    q_real = blocks[:tile_side, :tile_side] - blocks[tile_side:, tile_side:]
    q_imag = blocks[:tile_side, tile_side:] + blocks[tile_side:, :tile_side]
    merged = jnp.concatenate([q_real, q_imag], axis=0).astype(jnp.bfloat16)
    return jnp.dot(neg_table, merged, preferred_element_type=jnp.float32) / float(
        tile_side * tile_side
    )


def forward_single(source, cos_sin, stacked):
    real_part, imag_part = forward_batch(source[None], cos_sin, stacked)
    return (real_part[0], imag_part[0])


def filter_spectra(kernels, cos_full, sin_full):
    highest = lax.Precision.HIGHEST
    cos_top = cos_full[:FS, :]
    sin_top = sin_full[:FS, :]
    cos_left = cos_full[:, :FS]
    sin_left = sin_full[:, :FS]
    part_re = jnp.einsum(
        "kab,bg->kag", kernels, cos_top, precision=highest, preferred_element_type=jnp.float32
    )
    part_im = -jnp.einsum(
        "kab,bg->kag", kernels, sin_top, precision=highest, preferred_element_type=jnp.float32
    )
    spec_re = jnp.einsum(
        "fa,kag->kfg", cos_left, part_re, precision=highest, preferred_element_type=jnp.float32
    ) + jnp.einsum(
        "fa,kag->kfg", sin_left, part_im, precision=highest, preferred_element_type=jnp.float32
    )
    spec_im = jnp.einsum(
        "fa,kag->kfg", cos_left, part_im, precision=highest, preferred_element_type=jnp.float32
    ) - jnp.einsum(
        "fa,kag->kfg", sin_left, part_re, precision=highest, preferred_element_type=jnp.float32
    )
    return (spec_re, spec_im)


def crop_filters(spec_re, spec_im, cos_full, sin_full):
    highest = lax.Precision.HIGHEST
    tile_side = spec_re.shape[1]
    cos_top = cos_full[:FS, :]
    sin_top = sin_full[:FS, :]
    cos_left = cos_full[:, :FS]
    sin_left = sin_full[:, :FS]
    vec_re = jnp.einsum(
        "kfg,gb->kfb", spec_re, cos_left, precision=highest, preferred_element_type=jnp.float32
    ) - jnp.einsum(
        "kfg,gb->kfb", spec_im, sin_left, precision=highest, preferred_element_type=jnp.float32
    )
    vec_im = jnp.einsum(
        "kfg,gb->kfb", spec_re, sin_left, precision=highest, preferred_element_type=jnp.float32
    ) + jnp.einsum(
        "kfg,gb->kfb", spec_im, cos_left, precision=highest, preferred_element_type=jnp.float32
    )
    raw_filter = (
        jnp.einsum(
            "af,kfb->kab", cos_top, vec_re, precision=highest, preferred_element_type=jnp.float32
        )
        - jnp.einsum(
            "af,kfb->kab", sin_top, vec_im, precision=highest, preferred_element_type=jnp.float32
        )
    ) / float(tile_side * tile_side)
    rescale = lax.rsqrt(jnp.mean(raw_filter * raw_filter, axis=(1, 2), keepdims=True) + norm_eps)
    return (raw_filter * rescale).reshape(raw_filter.shape[0], FS * FS)


def body(code_maps, dual_maps, survey_tile, filters, valid_blocks):
    tile_side = survey_tile.shape[0]
    filt_count = code_maps.shape[0]
    cos_full, sin_full = dft_tables(tile_side)
    cos_b = cos_full.astype(jnp.bfloat16)
    sin_b = sin_full.astype(jnp.bfloat16)
    cos_sin = jnp.concatenate([cos_b, sin_b], axis=1)
    cos_sin_wide = cos_sin.astype(jnp.float32)
    stacked = jnp.concatenate([cos_b, sin_b], axis=0)
    neg_table = jnp.concatenate([cos_b, -sin_b], axis=1)
    dict_weight = dict_scale * float(tile_side * tile_side)
    kernels = filters.reshape(filt_count, FS, FS)
    d_re, d_im = filter_spectra(kernels, cos_full, sin_full)
    z_re, z_im = forward_batch(code_maps, cos_sin, stacked)
    code_gap = (code_maps.astype(jnp.float32) - dual_maps.astype(jnp.float32)).astype(jnp.bfloat16)
    g_re, g_im = forward_batch(code_gap, cos_sin, stacked)
    q_part_re = jnp.sum(d_re * z_re - d_im * z_im, axis=0)
    q_part_im = jnp.sum(d_re * z_im + d_im * z_re, axis=0)
    d_part = jnp.sum(d_re * d_re + d_im * d_im, axis=0)
    recon_in = (q_part_re, q_part_im, d_part)
    q_re, q_im, d_norm = lax.psum((recon_in[0], recon_in[1], recon_in[2]), "filt")
    rebuilt = inverse_exact(q_re, q_im, cos_sin_wide, neg_table)
    row_mask = jnp.repeat(valid_blocks, MB).astype(jnp.float32)[:, None]
    filled = row_mask * survey_tile + (1.0 - row_mask) * rebuilt
    s_re, s_im = forward_single(filled.astype(jnp.bfloat16), cos_sin, stacked)
    b_re = d_re * s_re + d_im * s_im + penalty * g_re
    b_im = d_re * s_im - d_im * s_re + penalty * g_im
    e_part_re = jnp.sum(d_re * b_re - d_im * b_im, axis=0)
    e_part_im = jnp.sum(d_re * b_im + d_im * b_re, axis=0)
    coupling_in = (e_part_re, e_part_im)
    e_re, e_im = lax.psum((coupling_in[0], coupling_in[1]), "filt")
    divisor = penalty + d_norm
    t_re = e_re / divisor
    t_im = e_im / divisor
    x_re = (b_re - (d_re * t_re + d_im * t_im)) / penalty
    x_im = (b_im - (d_re * t_im - d_im * t_re)) / penalty
    spatial = inverse_batch(
        x_re.astype(jnp.bfloat16), x_im.astype(jnp.bfloat16), cos_sin, neg_table
    )
    shifted = spatial + dual_maps.astype(jnp.float32)
    shrunk = jnp.sign(shifted) * jnp.maximum(jnp.abs(shifted) - shrink_level, 0.0)
    new_codes = shrunk.astype(jnp.bfloat16)
    new_duals = (shifted - shrunk).astype(jnp.bfloat16)
    c_re = x_re * s_re + x_im * s_im + dict_weight * d_re
    c_im = x_re * s_im - x_im * s_re + dict_weight * d_im
    own_den = dict_weight + x_re * x_re + x_im * x_im
    new_filters = crop_filters(c_re / own_den, c_im / own_den, cos_full, sin_full)
    return (new_codes, new_duals, new_filters)


def solution(mesh):
    return jax.shard_map(
        body,
        mesh=mesh,
        in_specs=(
            P("filt", "grp", None),
            P("filt", "grp", None),
            P("grp", None),
            P("filt", "grp"),
            P("grp"),
        ),
        out_specs=(P("filt", "grp", None), P("filt", "grp", None), P("filt", "grp")),
        check_vma=False,
    )
```

profile of v0, /device:TPU:0, one launch (start us, length us, event | category | flops | bytes accessed | tf_op | source)
XLA Modules:
  0.0 545.3 jit_solution(5812333881721488143)
XLA Ops:
  14.8 5.4 fusion.86
  21.4 8.1 %fusion.91 = f32[8,512,512]{1,2,0:T(8,128)S(1)} fusion(f32[8,11,512]{2,1,0:T(8,128)S(1)} %convolution_bitcast_fusion.3, f32[512,512]{1,0:T(8,128)S(1)} %fusion.85), kind=kOutput, calls=%fused_computation.141 | convolution fusion | flops 276824064 | bytes 8912896 | tf_op jit(solution)/shard_map/fa,kag->kfg/dot_general | solution.py:79
  29.9 10.9 %fusion.90 = f32[8,512,512]{1,2,0:T(8,128)} fusion(f32[8,11,512]{2,1,0:T(8,128)S(1)} %fusion.55, f32[512,512]{1,0:T(8,128)S(1)} %fusion.85), kind=kOutput, calls=%fused_computation.140 | convolution fusion | flops 276824064 | bytes 8912896 | tf_op jit(solution)/shard_map/fa,kag->kfg/dot_general | solution.py:84
  40.8 12.0 %convolution_add_fusion = f32[8,512,512]{1,2,0:T(8,128)} fusion(f32[8,512,512]{1,2,0:T(8,128)S(1)} %fusion.91, f32[8,11,512]{2,1,0:T(8,128)S(1)} %fusion.55, f32[512,512]{1,0:T(8,128)S(1)} %fusion.84), kind=kOutput, calls=%fused_computation.78 | convolution fusion | flops 278921216 | bytes 17301504 | tf_op jit(solution)/shard_map/fa,kag->kfg/dot_general | solution.py:81
  52.8 21.8 %convolution_bitcast_fusion.1 = f32[8,1024,1024]{2,1,0:T(8,128)} fusion(bf16[8,512,512]{2,1,0:T(8,128)(2,1)} %param.5, bf16[512,512]{1,0:T(8,128)(2,1)} %get-tuple-element.43, bf16[512,512]{1,0:T(8,128)(2,1)S(1)} %get-tuple-element.42), kind=kOutput, calls=%fused_computation.1 | convolution fusion | flops 12893290496 | bytes 38797312 | tf_op jit(solution)/shard_map/fi,kic->kfc/dot_general | solution.py:30
  74.6 23.5 %fusion.18 = (f32[512,512]{1,0:T(8,128)}, f32[512,512]{1,0:T(8,128)}, f32[8,512,512]{1,2,0:T(8,128)}) fusion(f32[8,512,512]{1,2,0:T(8,128)} %convolution_add_fusion, f32[8,1024,1024]{2,1,0:T(8,128)} %convolution_bitcast_fusion.1, f32[8,512,512]{1,2,0:T(8,128)} %fusion.90, f32[8,11,512]{2,1,0:T(8,128)S(1)} %convolution_bitcast_fusion.3, ...), kind=kOutput, calls=%fused_computation.38 | convolution fusion | flops 301465600 | bytes 61341696 | tf_op jit(solution)/shard_map/fa,kag->kfg/dot_general | solution.py:86
  98.2 6.5 %copy.29 = bf16[8,512,512]{1,2,0:T(8,128)(2,1)} copy(bf16[8,512,512]{2,1,0:T(8,128)(2,1)} %param.5) | data formatting | bytes 8388608 | tf_op args[0]
  104.7 6.4 %copy.30 = bf16[8,512,512]{1,2,0:T(8,128)(2,1)} copy(bf16[8,512,512]{2,1,0:T(8,128)(2,1)} %param.6) | data formatting | bytes 8388608 | tf_op args[1]
  111.2 21.7 %convolution_bitcast_fusion = f32[8,1024,1024]{2,1,0:T(8,128)} fusion(bf16[8,512,512]{1,2,0:T(8,128)(2,1)} %copy.30, bf16[8,512,512]{1,2,0:T(8,128)(2,1)} %copy.29, bf16[512,512]{1,0:T(8,128)(2,1)S(1)} %copy-done.5, bf16[512,512]{1,0:T(8,128)(2,1)S(1)} %get-tuple-element.42), kind=kOutput, calls=%fused_computation | convolution fusion | flops 12901679104 | bytes 42991616 | tf_op jit(solution)/shard_map/fi,kic->kfc/dot_general | solution.py:30
  137.2 97.8 %all-reduce.7.cloned.1.call-done = (f32[512,512]{1,0:T(8,128)}, f32[512,512]{1,0:T(8,128)}) async-done(((f32[512,512]{1,0:T(8,128)}, f32[512,512]{1,0:T(8,128)}), (f32[512,512]{1,0:T(8,128)}, f32[512,512]{1,0:T(8,128)})) %all-reduce.7.cloned.1.call-update) | async-done | bytes 2097168 | tf_op jit(solution)/shard_map/psum | solution.py:141
  235.0 5.1 fusion.49
  250.3 19.4 %fusion.24 = (f32[512,512]{1,0:T(8,128)}, f32[512,512]{1,0:T(8,128)}, f32[512,512]{1,0:T(8,128)}) fusion(f32[8,512,512]{1,2,0:T(8,128)} %get-tuple-element.39, f32[8,512,512]{1,2,0:T(8,128)} %convolution_add_fusion, f32[8,1024,1024]{2,1,0:T(8,128)} %convolution_bitcast_fusion, f32[512,512]{1,0:T(8,128)S(1)} %copy.28, f32[512,512]{1,0:T(8,128)S(1)} %copy.27), kind=kLoop, calls=%fused_computation.44 | loop fusion | flops 51642368 | bytes 55574528 | tf_op jit(solution)/shard_map/reduce_sum | solution.py:148
  274.9 132.6 %all-reduce.5.cloned.1.call-done = (f32[512,512]{1,0:T(8,128)}, f32[512,512]{1,0:T(8,128)}, f32[512,512]{1,0:T(8,128)}) async-done(((f32[512,512]{1,0:T(8,128)}, f32[512,512]{1,0:T(8,128)}, f32[512,512]{1,0:T(8,128)}), (f32[512,512]{1,0:T(8,128)}, f32[512,512]{1,0:T(8,128)}, f32[512,512]{1,0:T(8,128)})) %all-reduce.5.cloned.1.call-update) | async-done | bytes 3145744 | tf_op jit(solution)/shard_map/psum | solution.py:151
  409.9 26.9 %fusion.34 = (f32[8,512,512]{2,1,0:T(8,128)}, f32[8,512,512]{2,1,0:T(8,128)}, f32[8,512,512]{2,1,0:T(8,128)}) fusion(f32[8,512,512]{1,2,0:T(8,128)} %get-tuple-element.39, f32[512,512]{1,0:T(8,128)} %copy.33, f32[512,512]{1,0:T(8,128)} %copy.32, f32[512,512]{1,0:T(8,128)S(1)} %get-tuple-element.38, f32[512,512]{1,0:T(8,128)S(1)} %get-tuple-element.37, ...), kind=kLoop, calls=%fused_computation.54 | loop fusion | flops 69206016 | bytes 81788928 | tf_op jit(solution)/shard_map/div | solution.py:167
  436.9 12.0 %fusion.37 = (f32[8,512,512]{2,1,0:T(8,128)}, bf16[8,512,512]{2,1,0:T(8,128)(2,1)}, bf16[8,512,512]{2,1,0:T(8,128)(2,1)}) fusion(f32[8,512,512]{1,2,0:T(8,128)S(1)} %bitcast.206, f32[8,512,512]{2,1,0:T(8,128)} %get-tuple-element.21, f32[8,512,512]{2,1,0:T(8,128)} %get-tuple-element.20, f32[512,512]{1,0:T(8,128)} %copy.33, f32[512,512]{1,0:T(8,128)} %copy.32), kind=kLoop, calls=%fused_computation.67 | loop fusion | flops 29360128 | bytes 44040192 | tf_op jit(solution)/shard_map/div | solution.py:167
  448.8 9.9 %fusion.92 = f32[8,512,11]{1,2,0:T(8,128)S(1)} fusion(f32[8,512,512]{2,1,0:T(8,128)} %get-tuple-element.30, f32[512,512]{1,0:T(8,128)S(1)} %copy-done.2), kind=kOutput, calls=%fused_computation.142 | convolution fusion | flops 276824064 | bytes 8830976 | tf_op jit(solution)/shard_map/kfg,gb->kfb/dot_general | solution.py:104
  458.7 7.2 %fusion.89 = f32[8,512,11]{1,2,0:T(8,128)S(1)} fusion(f32[8,512,512]{2,1,0:T(8,128)S(1)} %copy-done, f32[512,512]{1,0:T(8,128)S(1)} %copy-done.4), kind=kOutput, calls=%fused_computation.139 | convolution fusion | flops 276824064 | bytes 8830976 | tf_op jit(solution)/shard_map/kfg,gb->kfb/dot_general | solution.py:99
  466.0 7.4 %convolution_add_fusion.1 = f32[8,512,11]{1,2,0:T(8,128)S(1)} fusion(f32[8,512,11]{1,2,0:T(8,128)S(1)} %fusion.92, f32[8,512,512]{2,1,0:T(8,128)S(1)} %bitcast.208, f32[512,512]{1,0:T(8,128)S(1)} %copy-done.4), kind=kOutput, calls=%fused_computation.94 | convolution fusion | flops 276869120 | bytes 9093120 | tf_op jit(solution)/shard_map/kfg,gb->kfb/dot_general | solution.py:106
  473.4 7.2 %convolution_subtract_fusion.1 = f32[8,512,11]{1,2,0:T(8,128)S(1)} fusion(f32[8,512,11]{1,2,0:T(8,128)S(1)} %fusion.89, f32[8,512,512]{2,1,0:T(8,128)S(1)} %bitcast.208, f32[512,512]{1,0:T(8,128)S(1)} %copy-done.2), kind=kOutput, calls=%fused_computation.95 | convolution fusion | flops 276869120 | bytes 9093120 | tf_op jit(solution)/shard_map/kfg,gb->kfb/dot_general | solution.py:101
  482.3 17.6 %fusion.9 = f32[8,1024,1024]{2,1,0:T(8,128)} fusion(bf16[8,512,512]{2,1,0:T(8,128)(2,1)} %get-tuple-element.32, bf16[8,512,512]{2,1,0:T(8,128)(2,1)} %get-tuple-element.31, bf16[512,512]{1,0:T(8,128)(2,1)S(1)} %get-tuple-element.42, bf16[512,512]{1,0:T(8,128)(2,1)} %get-tuple-element.43), kind=kOutput, calls=%fused_computation.19 | convolution fusion | flops 8608808960 | bytes 42991616 | tf_op jit(solution)/shard_map/kij,jc->kic/dot_general | solution.py:39
  499.9 12.6 %fusion.2 = (bf16[8,512,512]{2,1,0:T(8,128)(2,1)S(1)}, bf16[8,512,512]{2,1,0:T(8,128)(2,1)S(1)}) fusion(f32[8,1024,1024]{2,1,0:T(8,128)} %fusion.9), kind=kLoop, calls=%fused_computation.8 | loop fusion | flops 8388608 | bytes 41943040 | tf_op jit(solution)/shard_map/convert
  512.5 12.6 %subtract_convert_fusion = (bf16[8,512,512]{1,2,0:T(8,128)(2,1)}, bf16[8,512,512]{1,2,0:T(8,128)(2,1)}) fusion(bf16[8,512,512]{1,2,0:T(8,128)(2,1)} %copy.30, bf16[512,512]{1,0:T(8,128)(2,1)} %copy-done.6, bf16[512,512]{1,0:T(8,128)(2,1)S(1)} %get-tuple-element.42, bf16[8,512,512]{2,1,0:T(8,128)(2,1)S(1)} %get-tuple-element.27, ...), kind=kOutput, calls=%fused_computation.69 | convolution fusion | flops 4336910336 | bytes 22020096 | tf_op jit(solution)/shard_map/fi,kic->kfc/dot_general | solution.py:43
  525.2 6.4 %copy.35 = bf16[8,512,512]{2,1,0:T(8,128)(2,1)} copy(bf16[8,512,512]{1,2,0:T(8,128)(2,1)} %get-tuple-element.29) | data formatting | bytes 8388608
  531.6 6.4 %copy.36 = bf16[8,512,512]{2,1,0:T(8,128)(2,1)} copy(bf16[8,512,512]{1,2,0:T(8,128)(2,1)} %get-tuple-element.28) | data formatting | bytes 8388608
  (54 shorter events, 33.0 us)
Async XLA Ops:
  7.2 227.9 %all-reduce.7.cloned.1.call-start = ((), (), s32[]{:S(2)}) async-start(), calls=%async_computation.1 | async-start | bytes 4194304 | tf_op jit(solution)/shard_map/psum | solution.py:141
  11.0 29.8 %copy-start.3 = (f32[512,512]{1,0:T(8,128)}, f32[512,512]{1,0:T(8,128)S(1)}, u32[]{:S(2)}) copy-start(f32[512,512]{1,0:T(8,128)S(1)} %fusion.85) | copy-start | bytes 3145732
  14.8 59.8 %copy-start.1 = (f32[512,512]{1,0:T(8,128)}, f32[512,512]{1,0:T(8,128)S(1)}, u32[]{:S(2)}) copy-start(f32[512,512]{1,0:T(8,128)S(1)} %fusion.84) | copy-start | bytes 3145732
  98.2 13.0 %copy-start.5 = (bf16[512,512]{1,0:T(8,128)(2,1)S(1)}, bf16[512,512]{1,0:T(8,128)(2,1)}, u32[]{:S(2)}) copy-start(bf16[512,512]{1,0:T(8,128)(2,1)} %get-tuple-element.43) | copy-start | bytes 1572868
  98.2 309.3 %all-reduce.5.cloned.1.call-start = ((), (), s32[]{:S(2)}) async-start(), calls=%async_computation | async-start | bytes 6291456 | tf_op jit(solution)/shard_map/psum | solution.py:151
  111.2 21.7 %copy-start.7 = (s32[4]{0:T(128)S(1)}, s32[4]{0:T(128)}, u32[]{:S(2)}) copy-start(s32[4]{0:T(128)} %param.9) | copy-start | bytes 52
  137.1 106.9 %copy-start.6 = (bf16[512,512]{1,0:T(8,128)(2,1)}, bf16[512,512]{1,0:T(8,128)(2,1)S(1)}, u32[]{:S(2)}) copy-start(bf16[512,512]{1,0:T(8,128)(2,1)S(1)} %fusion.88) | copy-start | bytes 1572868
  407.5 29.3 %slice-start = ((s8[8388608]{0:T(1024)(128)(4,1)}), s8[4194304]{0:T(1024)(128)(4,1)S(1)}, s32[]{:S(2)}) async-start(s8[8388608]{0:T(1024)(128)(4,1)} %bitcast.205), calls=%async_computation.2 | async-start | bytes 8388608
  409.9 26.9 %slice-start.1 = ((s8[8388608]{0:T(1024)(128)(4,1)}), s8[4194304]{0:T(1024)(128)(4,1)S(1)}, s32[]{:S(2)}) async-start(s8[8388608]{0:T(1024)(128)(4,1)} %bitcast.205), calls=%async_computation.3 | async-start | bytes 8388608
  436.8 12.0 %copy-start.2 = (f32[512,512]{1,0:T(8,128)S(1)}, f32[512,512]{1,0:T(8,128)}, u32[]{:S(2)}) copy-start(f32[512,512]{1,0:T(8,128)} %copy-done.1) | copy-start | bytes 3145732
  436.8 21.9 %copy-start.4 = (f32[512,512]{1,0:T(8,128)S(1)}, f32[512,512]{1,0:T(8,128)}, u32[]{:S(2)}) copy-start(f32[512,512]{1,0:T(8,128)} %copy-done.3) | copy-start | bytes 3145732
  448.8 9.9 %copy-start = (f32[8,512,512]{2,1,0:T(8,128)S(1)}, f32[8,512,512]{2,1,0:T(8,128)}, u32[]{:S(2)}) copy-start(f32[8,512,512]{2,1,0:T(8,128)} %get-tuple-element.30) | copy-start | bytes 25165828
  448.8 17.1 %slice-start.2 = ((s8[8388608]{0:T(1024)(128)(4,1)}), s8[4194304]{0:T(1024)(128)(4,1)S(1)}, s32[]{:S(2)}) async-start(s8[8388608]{0:T(1024)(128)(4,1)} %bitcast.207), calls=%async_computation.4 | async-start | bytes 8388608
  458.7 7.2 %slice-start.3 = ((s8[8388608]{0:T(1024)(128)(4,1)}), s8[4194304]{0:T(1024)(128)(4,1)S(1)}, s32[]{:S(2)}) async-start(s8[8388608]{0:T(1024)(128)(4,1)} %bitcast.207), calls=%async_computation.5 | async-start | bytes 8388608
Sparse Core Ops, SparseCore 0:
  98.3 136.7 all-reduce.6
  269.9 137.5 all-reduce.4
where the time goes:
time: 552 us; the launch traced here: 545 us
  waiting for transfers between devices  230 us (42%)
  matrix products  173 us (31%)
  other arithmetic  92.9 us (17%)
  local copies, waits for them, and re-layouts  34.6 us (6%)
  between operations  14.7 us (3%)
    psum x1, waiting for transfers between devices, body(): e_re, e_im = lax.psum((coupling_in[0], coupling_in[1]), 'filt')  133 us
    psum x1, waiting for transfers between devices, body(): lax.psum((recon_in[0], recon_in[1], recon_in[2]), 'filt')  97.8 us
    dot_general x3, matrix products, forward_batch(): jnp.einsum('fi,kic->kfc', stacked, halves, preferred_element_type=jnp.flo...  46 us
    div x1, other arithmetic, body(): c_im / own_den  26.9 us
    unnamed x28, local copies, waits for them, and re-layouts  25.9 us
    dot_general x1, matrix products, filter_spectra(): jnp.einsum('fa,kag->kfg', sin_left, part_re, precision=highest, preferred...  23.5 us
    reduce_sum x1, other arithmetic, body(): e_part_re = jnp.sum(d_re * b_re - d_im * b_im, axis=0)  19.4 us
    dot_general x1, matrix products, inverse_batch(): jnp.einsum('kij,jc->kic', stack_in, cos_sin, preferred_element_type=jnp.f...  17.6 us
  transfers between devices with their start and end apart: 2, of which 2 were waited for; matrix products, arithmetic and copies ran while one was open for 8% of the time, Pallas kernels for 0%

commit v1 on v0

v1 whole, which is shorter than its diff:
```python
import math

import jax
import jax.numpy as jnp
import ml_dtypes
import numpy as np
from jax import lax
from jax.experimental import pallas as pl
from jax.experimental.pallas import tpu as pltpu
from jax.sharding import PartitionSpec as P

FS = 11
MB = 128
PAD = 16
TERMS = 6
TAPS = 32
SUB = 8
LANES = 128

penalty = 128.0
shrink_level = 1.0
dict_scale = 0.0625
norm_eps = 1e-06

VMEM_LIMIT = 60 * 1024 * 1024
BF = ml_dtypes.bfloat16


def split_np(a, parts):
    out, rest = [], np.asarray(a, np.float32)
    for _ in range(parts):
        piece = rest.astype(BF)
        out.append(piece)
        rest = rest - piece.astype(np.float32)
    return out


def make_tables(n):
    half = n // 2
    hr = half + PAD
    idx = np.arange(n)
    phases = (idx[:, None] * idx[None, :]) % n
    angles = phases.astype(np.float32) * np.float32(2.0 * math.pi / n)
    c, s = np.cos(angles).astype(np.float32), np.sin(angles).astype(np.float32)
    cb, sb = c.astype(BF), s.astype(BF)
    perm = np.concatenate([np.arange(half), [half], n - np.arange(1, half)])
    weight = np.full((half + 1,), 2.0, np.float32)
    weight[0] = weight[half] = 1.0

    s_pack = sb[:, :half].copy()
    s_pack[:, 0] = cb[:, half]
    first = np.concatenate([cb[:, :half], s_pack], axis=1)

    second = np.zeros((2 * hr, n), BF)
    second[: half + 1] = cb[: half + 1]
    second[hr : hr + half + 1] = sb[: half + 1]

    inv_first = np.concatenate([cb[perm], sb[perm]], axis=1)

    wf = weight[:half][None, :]
    ti_c = cb[:, :half].astype(np.float32) * wf
    ti_s = -sb[:, :half].astype(np.float32) * wf
    ti_s[:, 0] = cb[:, half].astype(np.float32)
    inv_second = (np.concatenate([ti_c, ti_s], axis=1) / float(n * n)).astype(BF)

    left = np.zeros((2 * hr, 2 * PAD), np.float32)
    left[: half + 1, :FS] = c[: half + 1, :FS]
    left[: half + 1, PAD : PAD + FS] = s[: half + 1, :FS]
    left[hr : hr + half + 1, :FS] = -s[: half + 1, :FS]
    left[hr : hr + half + 1, PAD : PAD + FS] = c[: half + 1, :FS]
    l0, l1, l2 = split_np(left, 3)
    left6 = np.concatenate([l0, l0, l1, l0, l1, l2], axis=1)
    top = np.concatenate([c[:FS][:, perm], -s[:FS][:, perm]], axis=1)

    crop = np.zeros((n, 128), BF)
    for at, table in ((0, c), (PAD, s)):
        hi, lo = split_np(table[perm][:, :FS], 2)
        crop[:, at : at + FS] = hi
        crop[:, 2 * PAD + at : 2 * PAD + at + FS] = lo
    rows = np.zeros((2 * PAD, 2 * hr), np.float32)
    wc = c[:FS, : half + 1] * weight[None, :]
    ws = s[:FS, : half + 1] * weight[None, :]
    rows[:FS, : half + 1] = wc
    rows[:FS, hr : hr + half + 1] = -ws
    rows[PAD : PAD + FS, : half + 1] = -ws
    rows[PAD : PAD + FS, hr : hr + half + 1] = -wc
    r_hi, r_lo = split_np(rows, 2)
    crop_rows = np.concatenate([r_hi, r_lo], axis=0)

    grid = np.arange(TAPS)
    turn = 2.0 * math.pi / TAPS
    a_of, b_of = np.divmod(np.arange(FS * FS), FS)
    ang = turn * ((a_of[:, None] * np.repeat(grid, TAPS)[None, :] + b_of[:, None] * np.tile(grid, TAPS)[None, :]) % TAPS)
    sample = np.concatenate([np.cos(ang), np.sin(ang)], axis=1).astype(np.float32)
    taps = np.arange(-(FS - 1), FS)

    def interp(freqs):
        diff = freqs[:, None] * (2.0 * math.pi / n) - grid[None, :] * turn
        return np.cos(diff[:, :, None] * taps[None, None, :]).sum(axis=2) / TAPS

    up_rows = np.zeros((hr, TAPS), np.float32)
    up_rows[: half + 1] = interp(np.arange(half + 1))
    up_cols = np.zeros((LANES, n), np.float32)
    up_cols[:TAPS] = interp(perm).T
    return dict(
        sample=sample, up_rows=up_rows, up_cols=up_cols,
        first=first, second=second, inv_first=inv_first, inv_second=inv_second,
        left6=left6, top=top, crop=crop, crop_rows=crop_rows,
    )


def mm(a, b):
    return jnp.dot(a, b, preferred_element_type=jnp.float32)


def spectrum_rows(y_ref, hr, half, r0, rb):
    rows, srows = pl.ds(r0, rb), pl.ds(hr + r0, rb)
    cc, cs = y_ref[rows, :half], y_ref[rows, half:]
    sc, ss = y_ref[srows, :half], y_ref[srows, half:]
    col0 = lax.broadcasted_iota(jnp.int32, (rb, half), 1) == 0
    zero = jnp.zeros_like(cc)
    plus = (cc - jnp.where(col0, zero, ss), -(sc + jnp.where(col0, zero, cs)))
    minus = (jnp.where(col0, cs, cc + ss), jnp.where(col0, -ss, cs - sc))
    return plus, minus


def sums_kernel(n, code_ref, dual_ref, td_ref, energy_ref, first_ref, second_ref, left_ref, acc_ref, b_ref, p_ref, yz_ref, yb_ref, d_ref):
    half = n // 2
    hr = half + PAD

    @pl.when(pl.program_id(0) == 0)
    def _():
        acc_ref[...] = jnp.zeros_like(acc_ref)

    code = code_ref[0]
    gap = (code.astype(jnp.float32) - dual_ref[0].astype(jnp.float32)).astype(jnp.bfloat16)
    d_ref[...] = mm(left_ref[...], td_ref[0])
    p_ref[0] = mm(code, first_ref[...]).astype(jnp.bfloat16)
    p_ref[1] = mm(gap, first_ref[...]).astype(jnp.bfloat16)
    yz_ref[...] = mm(second_ref[...], p_ref[0])
    yb_ref[...] = mm(second_ref[...], p_ref[1])
    rb = 2 * SUB
    for r0 in range(0, hr, rb):
        rows, srows = pl.ds(r0, rb), pl.ds(hr + r0, rb)
        z_halves = spectrum_rows(yz_ref, hr, half, r0, rb)
        b_halves = spectrum_rows(yb_ref, hr, half, r0, rb)
        for h in range(2):
            cols = slice(h * half, (h + 1) * half)
            d_re, d_im = d_ref[rows, cols], d_ref[srows, cols]
            z_re, z_im = z_halves[h]
            b_re, b_im = b_halves[h]
            b_ref[0, 0, rows, cols] = b_re
            b_ref[0, 1, rows, cols] = b_im
            terms = (
                d_re * z_re - d_im * z_im, d_re * z_im + d_im * z_re,
                d_re * b_re - d_im * b_im, d_re * b_im + d_im * b_re,
            )
            for part, term in enumerate(terms):
                for c in range(half // LANES):
                    at = tile_at(n, part, h * (half // LANES) + c, r0)
                    acc_ref[pl.ds(at, 2)] += term[:, c * LANES : (c + 1) * LANES].reshape(2, SUB, LANES)

    @pl.when(pl.program_id(0) == pl.num_programs(0) - 1)
    def _():
        for c in range(TAPS // SUB):
            acc_ref[tile_at(n, 0, c, hr - SUB)] = energy_ref[c]


def tile_at(n, part, group, row):
    return (part * (n // LANES) + group) * ((n // 2 + PAD) // SUB) + row // SUB


def load_rows(ref, n, part, r0, rb, first, last):
    pieces = [ref[pl.ds(tile_at(n, part, g, r0), rb // SUB)].reshape(rb, LANES) for g in range(first, last)]
    return jnp.concatenate(pieces, axis=1)


def sum_stages(devices):
    bits = devices.bit_length() - 1
    if devices != 1 << bits:
        raise ValueError("bad count")
    low = (bits - 1) // 2
    sizes = [1, low, bits - 1 - low] if bits else []
    stages, stride = [], 1
    for size in sizes:
        if size > 0:
            stages.append((1 << size, stride))
        stride <<= max(size, 0)
    return stages


def exchange_kernel(stages, lanes, x_ref, out_ref, sum_ref, recv_ref, rs_send, rs_recv, ag_send, ag_recv):
    me = lax.axis_index("filt")
    digits = [lax.rem(me // stride, radix) for radix, stride in stages]

    def peer_of(stage, digit):
        return me + (digit - digits[stage]) * stages[stage][1]

    barrier = pltpu.get_barrier_semaphore()
    count = 0
    for stage, (radix, _) in enumerate(stages):
        for d in range(1, radix):
            pl.semaphore_signal(
                barrier, inc=1, device_id={"filt": peer_of(stage, lax.rem(digits[stage] + d, radix))},
                device_id_type=pl.DeviceIdType.MESH,
            )
            count += 1
    pl.semaphore_wait(barrier, count)

    plans = []
    slot, sem = 0, 0
    for start, total, order in lanes:
        base, size, plan = start, total, []
        for position, stage in enumerate(order):
            radix = stages[stage][0]
            sub = size // radix
            plan.append((position, stage, radix, base, sub, slot, sem))
            base = base + digits[stage] * sub
            size = sub
            slot += (radix - 1) * sub
            sem += radix - 1
        plans.append(plan)

    def scatter(entry):
        position, stage, radix, base, sub, slot, sem = entry
        source = x_ref if position == 0 else sum_ref
        copies = []
        for d in range(1, radix):
            target = lax.rem(digits[stage] + d, radix)
            copies.append(pltpu.make_async_remote_copy(
                src_ref=source.at[pl.ds(base + target * sub, sub)],
                dst_ref=recv_ref.at[pl.ds(slot + (d - 1) * sub, sub)],
                send_sem=rs_send.at[sem + d - 1], recv_sem=rs_recv.at[sem + d - 1],
                device_id={"filt": peer_of(stage, target)}, device_id_type=pl.DeviceIdType.MESH,
            ))
        return copies

    def add_up(entry):
        position, stage, radix, base, sub, slot, sem = entry
        source = x_ref if position == 0 else sum_ref
        own = base + digits[stage] * sub
        result = out_ref if position == len(stages) - 1 else sum_ref
        step = max(w for w in range(1, 17) if sub % w == 0)

        def add(i, carry):
            value = source[pl.ds(own + i * step, step)]
            for d in range(1, radix):
                value = value + recv_ref[pl.ds(slot + (d - 1) * sub + i * step, step)]
            result[pl.ds(own + i * step, step)] = value
            return carry

        lax.fori_loop(0, sub // step, add, 0)

    def gather(entry):
        position, stage, radix, base, sub, slot, sem = entry
        own = pl.ds(base + digits[stage] * sub, sub)
        copies = []
        for d in range(1, radix):
            target = lax.rem(digits[stage] + d, radix)
            copies.append(pltpu.make_async_remote_copy(
                src_ref=out_ref.at[own], dst_ref=out_ref.at[own],
                send_sem=ag_send.at[sem + d - 1], recv_sem=ag_recv.at[sem + d - 1],
                device_id={"filt": peer_of(stage, target)}, device_id_type=pl.DeviceIdType.MESH,
            ))
        return copies

    depth = len(stages)
    flight = [None] * len(lanes)
    for step in range(2 * depth + 1):
        for lane in range(len(lanes)):
            if flight[lane] is not None:
                for copy in flight[lane]:
                    copy.wait()
                if step <= depth:
                    add_up(plans[lane][step - 1])
            if step < 2 * depth:
                entry = plans[lane][step if step < depth else 2 * depth - 1 - step]
                flight[lane] = scatter(entry) if step < depth else gather(entry)
                for copy in flight[lane]:
                    copy.start()


def fold_first(blk_ref, q_ref, n):
    half = n // 2
    hr = half + PAD
    rb = 16
    for r0 in range(0, half, rb):
        rows, srows = pl.ds(r0, rb), pl.ds(hr + r0, rb)
        q_re = blk_ref[rows, :n] - blk_ref[srows, n:]
        q_im = blk_ref[rows, n:] + blk_ref[srows, :n]
        if r0 == 0:
            last = blk_ref[half : half + 8, :n] - blk_ref[hr + half : hr + half + 8, n:]
            row0 = lax.broadcasted_iota(jnp.int32, (rb, n), 0) == 0
            q_im = jnp.where(row0, jnp.broadcast_to(last[0:1], (rb, n)), q_im)
        q_ref[rows, :] = q_re.astype(jnp.bfloat16)
        q_ref[pl.ds(half + r0, rb), :] = q_im.astype(jnp.bfloat16)


def update_kernel(
    n, sums_ref, up_rows_ref, up_cols_ref, survey_ref, mask_ref, b_ref, dual_ref, td_ref, first_ref, second_ref, inv_first_ref,
    inv_second_ref, left_ref, crop_ref, crop_rows_ref,
    codes_ref, duals_ref, raw_ref,
    s_ref, r_ref, d_ref, x_ref, e_ref, blk_ref, q_ref,
):
    half = n // 2
    hr = half + PAD
    rb = 16
    dict_weight = dict_scale * float(n * n)

    @pl.when(pl.program_id(0) == 0)
    def _():
        for r0 in range(0, hr, rb):
            rows, srows = pl.ds(r0, rb), pl.ds(hr + r0, rb)
            for part, at in ((0, rows), (1, srows)):
                v = load_rows(sums_ref, n, part, r0, rb, 0, n // LANES)
                hi = v.astype(jnp.bfloat16)
                rest = v - hi.astype(jnp.float32)
                mid = rest.astype(jnp.bfloat16)
                x_ref[at, :] = hi
                e_ref[pl.ds(part * hr + r0, rb), :] = mid
                e_ref[pl.ds((2 + part) * hr + r0, rb), :] = (rest - mid.astype(jnp.float32)).astype(jnp.bfloat16)
        blk_ref[...] = mm(x_ref[...], inv_first_ref[...])
        blk_ref[...] += mm(e_ref[: 2 * hr, :], inv_first_ref[...])
        blk_ref[...] += mm(e_ref[2 * hr :, :], inv_first_ref[...])
        fold_first(blk_ref, q_ref, n)
        rebuilt = mm(inv_second_ref[...], q_ref[...])
        m = mask_ref[...]
        filled = (m * survey_ref[...] + (1.0 - m) * rebuilt).astype(jnp.bfloat16)
        q_ref[...] = mm(filled, first_ref[...]).astype(jnp.bfloat16)
        d_ref[...] = mm(second_ref[...], q_ref[...])
        samples = jnp.concatenate([sums_ref[tile_at(n, 0, c, hr - SUB)] for c in range(TAPS // SUB)], axis=0)
        exact = dict(precision=lax.Precision.HIGHEST, preferred_element_type=jnp.float32)
        r_ref[0] = jnp.dot(jnp.dot(up_rows_ref[...], samples, **exact), up_cols_ref[...], **exact)
        for r0 in range(0, hr, rb):
            rows = pl.ds(r0, rb)
            halves = spectrum_rows(d_ref, hr, half, r0, rb)
            for h in range(2):
                cols = slice(h * half, (h + 1) * half)
                s_re, s_im = halves[h]
                scale = 1.0 / (penalty + jnp.maximum(r_ref[0, rows, cols], 0.0))
                g0, g1 = h * (half // LANES), (h + 1) * (half // LANES)
                s_ref[0, rows, cols] = s_re
                s_ref[1, rows, cols] = s_im
                r_ref[0, rows, cols] = (s_re - load_rows(sums_ref, n, 2, r0, rb, g0, g1)) * scale
                r_ref[1, rows, cols] = (s_im - load_rows(sums_ref, n, 3, r0, rb, g0, g1)) * scale

    d_ref[...] = mm(left_ref[...], td_ref[0])
    for r0 in range(0, hr, rb):
        rows, srows = pl.ds(r0, rb), pl.ds(hr + r0, rb)
        for h in range(2):
            cols = slice(h * half, (h + 1) * half)
            d_re, d_im = d_ref[rows, cols], d_ref[srows, cols]
            r_re, r_im = r_ref[0, rows, cols], r_ref[1, rows, cols]
            s_re, s_im = s_ref[0, rows, cols], s_ref[1, rows, cols]
            x_re = b_ref[0, 0, rows, cols] + (d_re * r_re + d_im * r_im)
            x_im = b_ref[0, 1, rows, cols] + (d_re * r_im - d_im * r_re)
            x_ref[rows, cols] = x_re.astype(jnp.bfloat16)
            x_ref[srows, cols] = x_im.astype(jnp.bfloat16)
            inv = 1.0 / (dict_weight + x_re * x_re + x_im * x_im)
            e_re = (x_re * s_re + x_im * s_im + dict_weight * d_re) * inv
            e_im = (x_re * s_im - x_im * s_re + dict_weight * d_im) * inv
            for part, e in ((0, e_re), (1, e_im)):
                hi = e.astype(jnp.bfloat16)
                e_ref[pl.ds(part * hr + r0, rb), cols] = hi
                e_ref[pl.ds((2 + part) * hr + r0, rb), cols] = (e - hi.astype(jnp.float32)).astype(jnp.bfloat16)
    blk_ref[...] = mm(x_ref[...], inv_first_ref[...])
    v = mm(e_ref[: 2 * hr, :], crop_ref[...]) + mm(e_ref[2 * hr :, :], crop_ref[...])
    v_hi = v.astype(jnp.bfloat16)
    v_lo = (v - v_hi.astype(jnp.float32)).astype(jnp.bfloat16)
    raw_ref[0] = mm(crop_rows_ref[...], v_hi) + mm(crop_rows_ref[...], v_lo)
    fold_first(blk_ref, q_ref, n)
    shifted = mm(inv_second_ref[...], q_ref[...]) + dual_ref[0].astype(jnp.float32)
    shrunk = shifted - jnp.clip(shifted, -shrink_level, shrink_level)
    codes_ref[0] = shrunk.astype(jnp.bfloat16)
    duals_ref[0] = (shifted - shrunk).astype(jnp.bfloat16)


def whole_spec(shape):
    return pl.BlockSpec(shape, lambda k: (0,) * len(shape))


def per_filter(shape):
    return pl.BlockSpec((1,) + shape, lambda k: (k,) + (0,) * len(shape))


def filter_terms(filters, top, n):
    count = filters.shape[0]
    kernels = filters.reshape(count, FS, FS)
    t = jnp.einsum("kab,bg->kag", kernels, top, precision=lax.Precision.HIGHEST, preferred_element_type=jnp.float32)
    gap = ((0, 0), (0, PAD - FS), (0, 0))
    t = jnp.concatenate([jnp.pad(t[:, :, :n], gap), jnp.pad(t[:, :, n:], gap)], axis=1)
    t0 = t.astype(jnp.bfloat16)
    rest = t - t0.astype(jnp.float32)
    t1 = rest.astype(jnp.bfloat16)
    t2 = (rest - t1.astype(jnp.float32)).astype(jnp.bfloat16)
    return jnp.concatenate([t0, t1, t0, t2, t1, t0], axis=1)


def energy_samples(filters, sample):
    spec = jnp.dot(filters, sample, precision=lax.Precision.HIGHEST, preferred_element_type=jnp.float32)
    energy = jnp.sum(spec * spec, axis=0).reshape(2, TAPS, TAPS).sum(axis=0)
    return jnp.pad(energy, ((0, 0), (0, LANES - TAPS))).reshape(TAPS // SUB, SUB, LANES)


def sum_plan(mesh, tiles):
    devices = mesh.shape["filt"]
    stages = sum_stages(devices)
    units = -(-tiles // devices)
    order = list(range(len(stages)))
    if len(stages) == 3 and units >= 4:
        other = max(1, (units * 4) // 17)
        rest = units - other
        sizes = [(rest + 2) // 3, other, (rest + 1) // 3, rest // 3]
        orders = [order, [0, 2, 1], order, order]
    else:
        sizes, orders = [units], [order]
    lanes, start = [], 0
    for size, own in zip(sizes, orders):
        lanes.append((start, size * devices, own))
        start += size * devices
    return stages, lanes, start


def reduce_tiles(acc, stages, lanes):
    if not stages:
        return acc
    room = 0
    for _, size, order in lanes:
        for stage in order:
            radix = stages[stage][0]
            size //= radix
            room += (radix - 1) * size
    sems = len(lanes) * sum(radix - 1 for radix, _ in stages)
    return pl.pallas_call(
        lambda *refs: exchange_kernel(stages, lanes, *refs),
        out_shape=jax.ShapeDtypeStruct(acc.shape, acc.dtype),
        in_specs=[pl.BlockSpec(memory_space=pltpu.VMEM)],
        out_specs=pl.BlockSpec(memory_space=pltpu.VMEM),
        scratch_shapes=[pltpu.VMEM(acc.shape, jnp.float32), pltpu.VMEM((room, SUB, LANES), jnp.float32)] + [pltpu.SemaphoreType.DMA((sems,))] * 4,
        compiler_params=pltpu.CompilerParams(collective_id=0, has_side_effects=True, vmem_limit_bytes=VMEM_LIMIT),
        name="exchange",
    )(acc)


def make_body(mesh):
    def body(code_maps, dual_maps, survey_tile, filters, valid_blocks):
        n = survey_tile.shape[0]
        count = code_maps.shape[0]
        hr = n // 2 + PAD
        t = make_tables(n)
        td = filter_terms(filters, t["top"], n)
        kdim = td.shape[1]
        f32, bf16 = jnp.float32, jnp.bfloat16
        params = pltpu.CompilerParams(vmem_limit_bytes=VMEM_LIMIT, dimension_semantics=("arbitrary",))
        stages, lanes, tiles = sum_plan(mesh, 4 * (n // LANES) * (hr // SUB))
        energy = energy_samples(filters, t["sample"])
        acc, b = pl.pallas_call(
            lambda *refs: sums_kernel(n, *refs),
            grid=(count,),
            in_specs=[per_filter((n, n)), per_filter((n, n)), per_filter((kdim, n)),
                      whole_spec((TAPS // SUB, SUB, LANES)), whole_spec((n, n)), whole_spec((2 * hr, n)), whole_spec((2 * hr, kdim))],
            out_specs=[whole_spec((tiles, SUB, LANES)), per_filter((2, hr, n))],
            out_shape=[jax.ShapeDtypeStruct((tiles, SUB, LANES), f32), jax.ShapeDtypeStruct((count, 2, hr, n), f32)],
            scratch_shapes=[pltpu.VMEM((2, n, n), bf16)] + [pltpu.VMEM((2 * hr, n), f32)] * 3,
            compiler_params=params,
            name="sums",
        )(code_maps, dual_maps, td, energy, t["first"], t["second"], t["left6"])
        sums = reduce_tiles(acc, stages, lanes)
        mask = jnp.repeat(valid_blocks, MB).astype(f32)[:, None]
        new_codes, new_duals, crops = pl.pallas_call(
            lambda *refs: update_kernel(n, *refs),
            grid=(count,),
            in_specs=[whole_spec((tiles, SUB, LANES)), whole_spec((hr, TAPS)), whole_spec((LANES, n)), whole_spec((n, n)), whole_spec((n, 1)), per_filter((2, hr, n)),
                      per_filter((n, n)), per_filter((kdim, n)), whole_spec((n, n)), whole_spec((2 * hr, n)),
                      whole_spec((n, 2 * n)), whole_spec((n, n)), whole_spec((2 * hr, kdim)),
                      whole_spec((n, 128)), whole_spec((4 * PAD, 2 * hr))],
            out_specs=[per_filter((n, n)), per_filter((n, n)), per_filter((4 * PAD, 128))],
            out_shape=[jax.ShapeDtypeStruct((count, n, n), bf16), jax.ShapeDtypeStruct((count, n, n), bf16),
                       jax.ShapeDtypeStruct((count, 4 * PAD, 128), f32)],
            scratch_shapes=[pltpu.VMEM((2, hr, n), f32), pltpu.VMEM((2, hr, n), f32), pltpu.VMEM((2 * hr, n), f32),
                            pltpu.VMEM((2 * hr, n), bf16), pltpu.VMEM((4 * hr, n), bf16),
                            pltpu.VMEM((2 * hr, 2 * n), f32), pltpu.VMEM((n, n), bf16)],
            compiler_params=params,
            name="update",
        )(sums, t["up_rows"], t["up_cols"], survey_tile, mask, b, dual_maps, td, t["first"], t["second"], t["inv_first"],
          t["inv_second"], t["left6"], t["crop"], t["crop_rows"])
        m = crops[:, : 2 * PAD] + crops[:, 2 * PAD :]
        m = m[:, :, : 2 * PAD] + m[:, :, 2 * PAD : 4 * PAD]
        raw = (m[:, :FS, :FS] + m[:, PAD : PAD + FS, PAD : PAD + FS]) / float(n * n)
        rescale = lax.rsqrt(jnp.mean(raw * raw, axis=(1, 2), keepdims=True) + norm_eps)
        return new_codes, new_duals, (raw * rescale).reshape(count, FS * FS)

    return body


def solution(mesh):
    return jax.shard_map(
        make_body(mesh),
        mesh=mesh,
        in_specs=(
            P("filt", "grp", None),
            P("filt", "grp", None),
            P("grp", None),
            P("filt", "grp"),
            P("grp"),
        ),
        out_specs=(P("filt", "grp", None), P("filt", "grp", None), P("filt", "grp")),
        check_vma=False,
    )
```

time: 552 us -> 96.3 us (0.17); the launches traced: 545 us -> 96 us
  waiting for transfers between devices: 230 us -> 0 us
  matrix products: 173 us -> 2.5 us
  other arithmetic: 92.9 us -> 2.39 us
  Pallas kernels: 0 us -> 86.1 us
  local copies, waits for them, and re-layouts: 34.6 us -> 4.26 us
  between operations: 14.7 us -> 0.76 us
    psum x2 -> x0, waiting for transfers between devices: 230 us -> none  [the longest x1 133 us: body(): e_re, e_im = lax.psum((coupling_in[0], coupling_in[1]), 'filt')]
    dot_general x19 -> x2, matrix products: 173 us -> 2.5 us  [the longest x1 1.94 us: energy_samples(): jnp.dot(filters, sample, precision=lax.Precision.HIGHEST, preferred_eleme...]
    pallas_call x0 -> x3, Pallas kernels: none -> 86.1 us  [the longest x1 38.5 us: reduce_tiles(): pl.pallas_call(lambda *refs: exchange_kernel(stages, lanes, *refs), out_s...]
    div x3 -> x0, other arithmetic: 41.2 us -> none  [the longest x1 26.9 us: body(): c_im / own_den]
    unnamed x28 -> x4, local copies, waits for them, and re-layouts: 25.9 us -> 1.17 us
    reduce_sum x1 -> x2, other arithmetic: 19.4 us -> 0.23 us  [the longest x1 0.21 us: body(): jnp.mean(raw * raw, axis=(1, 2), keepdims=True) + norm_eps]
    another operation x2 -> x0, other arithmetic: 13 us -> none
    mul x5 -> x0, local copies, waits for them, and re-layouts: 7.16 us -> none  [the longest x2 5.14 us: body(): c_re = x_re * s_re + x_im * s_im + dict_weight * d_re]
  transfers between devices with their start and end apart: 2 -> 0, of which waited for: 2 -> 0; matrix products, arithmetic and copies ran while one was open for 8% -> 0% of each run, Pallas kernels for 0% -> 0%
where the time goes in v1:
time: 96.3 us; the launch traced here: 96 us
  Pallas kernels  86.1 us (89%)
  local copies, waits for them, and re-layouts  4.26 us (4%)
  matrix products  2.5 us (3%)
  other arithmetic  2.39 us (2%)
    pallas_call x1, Pallas kernels, reduce_tiles(): pl.pallas_call(lambda *refs: exchange_kernel(stages, lanes, *refs), out_s...  38.5 us
    pallas_call x1, Pallas kernels, body(): pl.pallas_call(lambda *refs: update_kernel(n, *refs), grid=(count,), in_s...  29.9 us
    pallas_call x1, Pallas kernels, body(): pl.pallas_call(lambda *refs: sums_kernel(n, *refs), grid=(count,), in_spe...  17.6 us
    dot_general x1, matrix products, energy_samples(): jnp.dot(filters, sample, precision=lax.Precision.HIGHEST, preferred_eleme...  1.94 us

profile of v1, /device:TPU:0, one launch (start us, length us, event | category | flops | bytes accessed | tf_op | source)
XLA Modules:
  0.0 96.0 jit_solution(6427182019723907495)
XLA Ops:
  0.6 0.0 copy-start.1
  0.6 0.7 convert_element_type.39
  1.3 0.1 broadcast_in_dim.2
  1.4 1.9 %fusion = f32[2048]{0:T(1024)S(1)} fusion(f32[121,2048]{1,0:T(8,128)} %constant.35.clone, f32[8,121]{1,0:T(8,128)} %param.19), kind=kOutput, calls=%fused_computation.2 | convolution fusion | flops 23820288 | bytes 1003296 | tf_op jit(solution)/shard_map/dot_general | solution.py:400
  3.4 0.1 reshape.39
  3.4 0.6 pad_bitcast_fusion.refs_3_
  4.1 0.8 reshape.38
  4.8 0.9 copy.20.refs_4_
  5.7 0.0 copy-done.1
  5.7 0.6 convolution_bitcast_fusion
  6.3 0.1 fusion.3
  6.4 0.1 fusion.2
  6.5 0.1 fusion.4
  6.6 0.0 copy-start
  6.6 1.2 %copy-done = bf16[8,192,512]{2,1,0:T(8,128)(2,1)} copy-done((bf16[8,192,512]{2,1,0:T(8,128)(2,1)}, bf16[8,192,512]{2,1,0:T(8,128)(2,1)S(1)}, u32[]{:S(2)}) %copy-start) | copy-done | bytes 1572888
  7.8 17.6 %sums.1 = (f32[544,8,128]{2,1,0:T(8,128)}, f32[8,2,272,512]{3,2,1,0:T(8,128)}) custom-call(bf16[8,512,512]{2,1,0:T(8,128)(2,1)} %refs_0_.1, bf16[8,512,512]{2,1,0:T(8,128)(2,1)} %refs_6_.2, bf16[8,192,512]{2,1,0:T(8,128)(2,1)} %copy-done, f32[4,8,128]{2,1,0:T(8,128)} %pad_bitcast_fusion.refs_3_, bf16[512,512]{1,0:T(8,128)(2,1)} %constant.36.clone.refs_4_.refs_8_, ...), custom_call_target="tpu_custom_call" | custom-call | tf_op jit(solution)/shard_map/sums/pallas_call | solution.py:457
  25.4 38.5 %exchange.1.refs_0_ = f32[544,8,128]{2,1,0:T(8,128)} custom-call(f32[544,8,128]{2,1,0:T(8,128)} %get-tuple-element.8.refs_0_), custom_call_target="tpu_custom_call" | custom-call | tf_op jit(solution)/shard_map/exchange/pallas_call | solution.py:434
  64.0 29.9 %update.1 = (bf16[8,512,512]{2,1,0:T(8,128)(2,1)}, bf16[8,512,512]{2,1,0:T(8,128)(2,1)}, f32[8,64,128]{2,1,0:T(8,128)}) custom-call(f32[544,8,128]{2,1,0:T(8,128)} %exchange.1.refs_0_, f32[272,32]{1,0:T(8,128)} %constant.39.clone.refs_1_, f32[128,512]{1,0:T(8,128)} %constant.40.clone.refs_2_, f32[512,512]{1,0:T(8,128)} %refs_3_.1, f32[512,1]{1,0:T(8,128)} %copy.20.refs_4_, ...), custom_call_target="tpu_custom_call" | custom-call | tf_op jit(solution)/shard_map/update/pallas_call | solution.py:470
  93.9 1.0 %slice_add_fusion.1 = f32[8,32,128]{2,1,0:T(8,128)S(1)} fusion(f32[8,64,128]{2,1,0:T(8,128)} %get-tuple-element.12), kind=kLoop, calls=%fused_computation.16 | loop fusion | flops 32768 | bytes 393216 | tf_op jit(solution)/shard_map/add | solution.py:487
  94.9 0.1 slice_add_fusion
  95.0 0.2 multiply_reduce_fusion
  95.2 0.1 broadcast_multiply_fusion
  95.3 0.7 reshape.41
  (6 shorter events, 0.2 us)
Async XLA Ops:
  0.6 5.1 %copy-start.1 = (f32[11,1024,1]{1,0,2:T(8,128)S(1)}, f32[11,1024,1]{1,0,2:T(8,128)}, u32[]{:S(2)}) copy-start(f32[11,1024,1]{1,0,2:T(8,128)} %constant.54) | copy-start | bytes 135172
  6.6 1.2 %copy-start = (bf16[8,192,512]{2,1,0:T(8,128)(2,1)}, bf16[8,192,512]{2,1,0:T(8,128)(2,1)S(1)}, u32[]{:S(2)}) copy-start(bf16[8,192,512]{2,1,0:T(8,128)(2,1)S(1)} %convert_dynamic-update-slice_fusion.2.refs_2_.refs_7_) | copy-start | bytes 4718596

commit v2 on v1

--- a/solution.py
+++ b/solution.py
@@ -15,6 +15,8 @@
 TERMS = 6
 TAPS = 32
 SUB = 8
+SUM_FILTERS = 1
+UPDATE_FILTERS = 2
 LANES = 128
 
 penalty = 128.0
@@ -124,50 +126,96 @@
     return plus, minus
 
 
-def sums_kernel(n, code_ref, dual_ref, td_ref, energy_ref, first_ref, second_ref, left_ref, acc_ref, b_ref, p_ref, yz_ref, yb_ref, d_ref):
+def missing_blocks(valid_ref):
+    first = jnp.where(valid_ref[0] == 0, 0, jnp.where(valid_ref[1] == 0, 1, 2))
+    last = jnp.where(valid_ref[3] == 0, 3, jnp.where(valid_ref[2] == 0, 2, 1))
+    return [pl.ds(pl.multiple_of(at * MB, MB), MB) for at in (first, last)]
+
+
+def sums_kernel(
+    n, valid_ref, code_ref, dual_ref, td_ref, energy_ref, first_ref, second_ref, left_ref, inv_first_ref, inv_second_ref,
+    acc_ref, b_ref, p_ref, yz_ref, yb_ref, d_ref, q_ref, terms_ref, blk_ref, fold_ref,
+):
     half = n // 2
     hr = half + PAD
 
     @pl.when(pl.program_id(0) == 0)
     def _():
         acc_ref[...] = jnp.zeros_like(acc_ref)
-
-    code = code_ref[0]
-    gap = (code.astype(jnp.float32) - dual_ref[0].astype(jnp.float32)).astype(jnp.bfloat16)
-    d_ref[...] = mm(left_ref[...], td_ref[0])
-    p_ref[0] = mm(code, first_ref[...]).astype(jnp.bfloat16)
-    p_ref[1] = mm(gap, first_ref[...]).astype(jnp.bfloat16)
-    yz_ref[...] = mm(second_ref[...], p_ref[0])
-    yb_ref[...] = mm(second_ref[...], p_ref[1])
+        q_ref[...] = jnp.zeros_like(q_ref)
+
+    per = code_ref.shape[0]
     rb = 2 * SUB
-    for r0 in range(0, hr, rb):
-        rows, srows = pl.ds(r0, rb), pl.ds(hr + r0, rb)
-        z_halves = spectrum_rows(yz_ref, hr, half, r0, rb)
-        b_halves = spectrum_rows(yb_ref, hr, half, r0, rb)
-        for h in range(2):
-            cols = slice(h * half, (h + 1) * half)
-            d_re, d_im = d_ref[rows, cols], d_ref[srows, cols]
-            z_re, z_im = z_halves[h]
-            b_re, b_im = b_halves[h]
-            b_ref[0, 0, rows, cols] = b_re
-            b_ref[0, 1, rows, cols] = b_im
-            terms = (
-                d_re * z_re - d_im * z_im, d_re * z_im + d_im * z_re,
-                d_re * b_re - d_im * b_im, d_re * b_im + d_im * b_re,
-            )
-            for part, term in enumerate(terms):
-                for c in range(half // LANES):
-                    at = tile_at(n, part, h * (half // LANES) + c, r0)
-                    acc_ref[pl.ds(at, 2)] += term[:, c * LANES : (c + 1) * LANES].reshape(2, SUB, LANES)
+
+    def first_sections(j):
+        code = code_ref[j]
+        gap = (code.astype(jnp.float32) - dual_ref[j].astype(jnp.float32)).astype(jnp.bfloat16)
+        p_ref[j, 0] = mm(code, first_ref[...]).astype(jnp.bfloat16)
+        p_ref[j, 1] = mm(gap, first_ref[...]).astype(jnp.bfloat16)
+
+    def second_sections(j):
+        d_ref[j] = mm(left_ref[...], td_ref[j])
+        yz_ref[j] = mm(second_ref[...], p_ref[j, 0])
+        yb_ref[j] = mm(second_ref[...], p_ref[j, 1])
+
+    def add_products(j):
+        for r0 in range(0, hr, rb):
+            rows, srows = pl.ds(r0, rb), pl.ds(hr + r0, rb)
+            z_halves = spectrum_rows(yz_ref.at[j], hr, half, r0, rb)
+            b_halves = spectrum_rows(yb_ref.at[j], hr, half, r0, rb)
+            for h in range(2):
+                cols = slice(h * half, (h + 1) * half)
+                d_re, d_im = d_ref[j, rows, cols], d_ref[j, srows, cols]
+                z_re, z_im = z_halves[h]
+                b_re, b_im = b_halves[h]
+                b_ref[j, 0, rows, cols] = b_re
+                b_ref[j, 1, rows, cols] = b_im
+                q_ref[0, rows, cols] += d_re * z_re - d_im * z_im
+                q_ref[1, rows, cols] += d_re * z_im + d_im * z_re
+                for part, term in enumerate((d_re * b_re - d_im * b_im, d_re * b_im + d_im * b_re)):
+                    for c in range(half // LANES):
+                        at = tile_at(n, part, h * (half // LANES) + c, r0)
+                        acc_ref[pl.ds(at, 2)] += term[:, c * LANES : (c + 1) * LANES].reshape(2, SUB, LANES)
+
+    first_sections(0)
+    for j in range(per):
+        second_sections(j)
+        if j + 1 < per:
+            first_sections(j + 1)
+        if j > 0:
+            add_products(j - 1)
+    add_products(per - 1)
 
     @pl.when(pl.program_id(0) == pl.num_programs(0) - 1)
     def _():
         for c in range(TAPS // SUB):
             acc_ref[tile_at(n, 0, c, hr - SUB)] = energy_ref[c]
+        for r0 in range(0, hr, rb):
+            for part in range(2):
+                v = q_ref[part, pl.ds(r0, rb), :]
+                at = pl.ds(part * hr + r0, rb)
+                for term in range(3):
+                    piece = v.astype(jnp.bfloat16)
+                    terms_ref[term, at, :] = piece
+                    v = v - piece.astype(jnp.float32)
+        blk_ref[...] = mm(terms_ref[0], inv_first_ref[...])
+        blk_ref[...] += mm(terms_ref[1], inv_first_ref[...])
+        blk_ref[...] += mm(terms_ref[2], inv_first_ref[...])
+        fold_first(blk_ref, fold_ref.at[0], n, fold_ref.at[1])
+        for i, block in enumerate(missing_blocks(valid_ref)):
+            table = inv_second_ref[block, :]
+            part = mm(table, fold_ref[0]) + mm(table, fold_ref[1])
+            for c in range(n // LANES):
+                at = rebuilt_at(n, c, i * MB)
+                acc_ref[pl.ds(at, MB // SUB)] = part[:, c * LANES : (c + 1) * LANES].reshape(MB // SUB, SUB, LANES)
 
 
 def tile_at(n, part, group, row):
     return (part * (n // LANES) + group) * ((n // 2 + PAD) // SUB) + row // SUB
+
+
+def rebuilt_at(n, group, row):
+    return tile_at(n, 2, 0, 0) + (group * (n // 2) + row) // SUB
 
 
 def load_rows(ref, n, part, r0, rb, first, last):
@@ -280,7 +328,7 @@
                     copy.start()
 
 
-def fold_first(blk_ref, q_ref, n):
+def fold_first(blk_ref, q_ref, n, rest_ref=None):
     half = n // 2
     hr = half + PAD
     rb = 16
@@ -292,16 +340,20 @@
             last = blk_ref[half : half + 8, :n] - blk_ref[hr + half : hr + half + 8, n:]
             row0 = lax.broadcasted_iota(jnp.int32, (rb, n), 0) == 0
             q_im = jnp.where(row0, jnp.broadcast_to(last[0:1], (rb, n)), q_im)
-        q_ref[rows, :] = q_re.astype(jnp.bfloat16)
-        q_ref[pl.ds(half + r0, rb), :] = q_im.astype(jnp.bfloat16)
+        for at, q in ((rows, q_re), (pl.ds(half + r0, rb), q_im)):
+            hi = q.astype(jnp.bfloat16)
+            q_ref[at, :] = hi
+            if rest_ref is not None:
+                rest_ref[at, :] = (q - hi.astype(jnp.float32)).astype(jnp.bfloat16)
 
 
 def update_kernel(
-    n, sums_ref, up_rows_ref, up_cols_ref, survey_ref, mask_ref, b_ref, dual_ref, td_ref, first_ref, second_ref, inv_first_ref,
+    n, valid_ref, sums_ref, up_rows_ref, up_cols_ref, survey_ref, b_ref, dual_ref, td_ref, first_ref, second_ref, inv_first_ref,
     inv_second_ref, left_ref, crop_ref, crop_rows_ref,
     codes_ref, duals_ref, raw_ref,
-    s_ref, r_ref, d_ref, x_ref, e_ref, blk_ref, q_ref,
+    s_ref, r_ref, dj_ref, xj_ref, ej_ref, blkj_ref, qj_ref,
 ):
+    d_ref, x_ref, q_ref = dj_ref.at[0], xj_ref.at[0], qj_ref.at[0]
     half = n // 2
     hr = half + PAD
     rb = 16
@@ -309,24 +361,12 @@
 
     @pl.when(pl.program_id(0) == 0)
     def _():
-        for r0 in range(0, hr, rb):
-            rows, srows = pl.ds(r0, rb), pl.ds(hr + r0, rb)
-            for part, at in ((0, rows), (1, srows)):
-                v = load_rows(sums_ref, n, part, r0, rb, 0, n // LANES)
-                hi = v.astype(jnp.bfloat16)
-                rest = v - hi.astype(jnp.float32)
-                mid = rest.astype(jnp.bfloat16)
-                x_ref[at, :] = hi
-                e_ref[pl.ds(part * hr + r0, rb), :] = mid
-                e_ref[pl.ds((2 + part) * hr + r0, rb), :] = (rest - mid.astype(jnp.float32)).astype(jnp.bfloat16)
-        blk_ref[...] = mm(x_ref[...], inv_first_ref[...])
-        blk_ref[...] += mm(e_ref[: 2 * hr, :], inv_first_ref[...])
-        blk_ref[...] += mm(e_ref[2 * hr :, :], inv_first_ref[...])
-        fold_first(blk_ref, q_ref, n)
-        rebuilt = mm(inv_second_ref[...], q_ref[...])
-        m = mask_ref[...]
-        filled = (m * survey_ref[...] + (1.0 - m) * rebuilt).astype(jnp.bfloat16)
-        q_ref[...] = mm(filled, first_ref[...]).astype(jnp.bfloat16)
+        x_ref[:n, :] = survey_ref[...].astype(jnp.bfloat16)
+        for i, block in enumerate(missing_blocks(valid_ref)):
+            for c in range(n // LANES):
+                tiles = sums_ref[pl.ds(rebuilt_at(n, c, i * MB), MB // SUB)]
+                x_ref[block, c * LANES : (c + 1) * LANES] = tiles.reshape(MB, LANES).astype(jnp.bfloat16)
+        q_ref[...] = mm(x_ref[:n, :], first_ref[...]).astype(jnp.bfloat16)
         d_ref[...] = mm(second_ref[...], q_ref[...])
         samples = jnp.concatenate([sums_ref[tile_at(n, 0, c, hr - SUB)] for c in range(TAPS // SUB)], axis=0)
         exact = dict(precision=lax.Precision.HIGHEST, preferred_element_type=jnp.float32)
@@ -341,46 +381,66 @@
                 g0, g1 = h * (half // LANES), (h + 1) * (half // LANES)
                 s_ref[0, rows, cols] = s_re
                 s_ref[1, rows, cols] = s_im
-                r_ref[0, rows, cols] = (s_re - load_rows(sums_ref, n, 2, r0, rb, g0, g1)) * scale
-                r_ref[1, rows, cols] = (s_im - load_rows(sums_ref, n, 3, r0, rb, g0, g1)) * scale
-
-    d_ref[...] = mm(left_ref[...], td_ref[0])
-    for r0 in range(0, hr, rb):
-        rows, srows = pl.ds(r0, rb), pl.ds(hr + r0, rb)
-        for h in range(2):
-            cols = slice(h * half, (h + 1) * half)
-            d_re, d_im = d_ref[rows, cols], d_ref[srows, cols]
-            r_re, r_im = r_ref[0, rows, cols], r_ref[1, rows, cols]
-            s_re, s_im = s_ref[0, rows, cols], s_ref[1, rows, cols]
-            x_re = b_ref[0, 0, rows, cols] + (d_re * r_re + d_im * r_im)
-            x_im = b_ref[0, 1, rows, cols] + (d_re * r_im - d_im * r_re)
-            x_ref[rows, cols] = x_re.astype(jnp.bfloat16)
-            x_ref[srows, cols] = x_im.astype(jnp.bfloat16)
-            inv = 1.0 / (dict_weight + x_re * x_re + x_im * x_im)
-            e_re = (x_re * s_re + x_im * s_im + dict_weight * d_re) * inv
-            e_im = (x_re * s_im - x_im * s_re + dict_weight * d_im) * inv
-            for part, e in ((0, e_re), (1, e_im)):
-                hi = e.astype(jnp.bfloat16)
-                e_ref[pl.ds(part * hr + r0, rb), cols] = hi
-                e_ref[pl.ds((2 + part) * hr + r0, rb), cols] = (e - hi.astype(jnp.float32)).astype(jnp.bfloat16)
-    blk_ref[...] = mm(x_ref[...], inv_first_ref[...])
-    v = mm(e_ref[: 2 * hr, :], crop_ref[...]) + mm(e_ref[2 * hr :, :], crop_ref[...])
-    v_hi = v.astype(jnp.bfloat16)
-    v_lo = (v - v_hi.astype(jnp.float32)).astype(jnp.bfloat16)
-    raw_ref[0] = mm(crop_rows_ref[...], v_hi) + mm(crop_rows_ref[...], v_lo)
-    fold_first(blk_ref, q_ref, n)
-    shifted = mm(inv_second_ref[...], q_ref[...]) + dual_ref[0].astype(jnp.float32)
-    shrunk = shifted - jnp.clip(shifted, -shrink_level, shrink_level)
-    codes_ref[0] = shrunk.astype(jnp.bfloat16)
-    duals_ref[0] = (shifted - shrunk).astype(jnp.bfloat16)
+                r_ref[0, rows, cols] = (s_re - load_rows(sums_ref, n, 0, r0, rb, g0, g1)) * scale
+                r_ref[1, rows, cols] = (s_im - load_rows(sums_ref, n, 1, r0, rb, g0, g1)) * scale
+
+    per = dual_ref.shape[0]
+
+    def quotients(j):
+        dj_ref[j] = mm(left_ref[...], td_ref[j])
+        for r0 in range(0, hr, rb):
+            rows, srows = pl.ds(r0, rb), pl.ds(hr + r0, rb)
+            for h in range(2):
+                cols = slice(h * half, (h + 1) * half)
+                d_re, d_im = dj_ref[j, rows, cols], dj_ref[j, srows, cols]
+                r_re, r_im = r_ref[0, rows, cols], r_ref[1, rows, cols]
+                s_re, s_im = s_ref[0, rows, cols], s_ref[1, rows, cols]
+                x_re = b_ref[j, 0, rows, cols] + (d_re * r_re + d_im * r_im)
+                x_im = b_ref[j, 1, rows, cols] + (d_re * r_im - d_im * r_re)
+                xj_ref[j, rows, cols] = x_re.astype(jnp.bfloat16)
+                xj_ref[j, srows, cols] = x_im.astype(jnp.bfloat16)
+                den = dict_weight + x_re * x_re + x_im * x_im
+                inv = pl.reciprocal(den, approx=True)
+                inv = inv * (2.0 - den * inv)
+                e_re = (x_re * s_re + x_im * s_im + dict_weight * d_re) * inv
+                e_im = (x_re * s_im - x_im * s_re + dict_weight * d_im) * inv
+                for part, e in ((0, e_re), (1, e_im)):
+                    hi = e.astype(jnp.bfloat16)
+                    ej_ref[j, pl.ds(part * hr + r0, rb), cols] = hi
+                    ej_ref[j, pl.ds((2 + part) * hr + r0, rb), cols] = (e - hi.astype(jnp.float32)).astype(jnp.bfloat16)
+
+    def first_sections(j):
+        blkj_ref[j] = mm(xj_ref[j], inv_first_ref[...])
+        v = mm(ej_ref[j, : 2 * hr, :], crop_ref[...]) + mm(ej_ref[j, 2 * hr :, :], crop_ref[...])
+        v_hi = v.astype(jnp.bfloat16)
+        v_lo = (v - v_hi.astype(jnp.float32)).astype(jnp.bfloat16)
+        raw_ref[j] = mm(crop_rows_ref[...], v_hi) + mm(crop_rows_ref[...], v_lo)
+
+    def finish(j):
+        fold_first(blkj_ref.at[j], qj_ref.at[j], n)
+        shifted = mm(inv_second_ref[...], qj_ref[j]) + dual_ref[j].astype(jnp.float32)
+        shrunk = shifted - jnp.clip(shifted, -shrink_level, shrink_level)
+        codes_ref[j] = shrunk.astype(jnp.bfloat16)
+        duals_ref[j] = (shifted - shrunk).astype(jnp.bfloat16)
+
+    quotients(0)
+    for j in range(per):
+        first_sections(j)
+        if j + 1 < per:
+            quotients(j + 1)
+        finish(j)
 
 
 def whole_spec(shape):
     return pl.BlockSpec(shape, lambda k: (0,) * len(shape))
 
 
-def per_filter(shape):
-    return pl.BlockSpec((1,) + shape, lambda k: (k,) + (0,) * len(shape))
+def per_filter(per, shape):
+    return pl.BlockSpec((per,) + shape, lambda k: (k,) + (0,) * len(shape))
+
+
+def filters_per_step(count, most):
+    return max(w for w in range(1, most + 1) if count % w == 0)
 
 
 def filter_terms(filters, top, n):
@@ -452,37 +512,40 @@
         kdim = td.shape[1]
         f32, bf16 = jnp.float32, jnp.bfloat16
         params = pltpu.CompilerParams(vmem_limit_bytes=VMEM_LIMIT, dimension_semantics=("arbitrary",))
-        stages, lanes, tiles = sum_plan(mesh, 4 * (n // LANES) * (hr // SUB))
+        stages, lanes, tiles = sum_plan(mesh, rebuilt_at(n, n // LANES, 0))
         energy = energy_samples(filters, t["sample"])
+        per = filters_per_step(count, SUM_FILTERS)
         acc, b = pl.pallas_call(
             lambda *refs: sums_kernel(n, *refs),
-            grid=(count,),
-            in_specs=[per_filter((n, n)), per_filter((n, n)), per_filter((kdim, n)),
-                      whole_spec((TAPS // SUB, SUB, LANES)), whole_spec((n, n)), whole_spec((2 * hr, n)), whole_spec((2 * hr, kdim))],
-            out_specs=[whole_spec((tiles, SUB, LANES)), per_filter((2, hr, n))],
+            grid=(count // per,),
+            in_specs=[pl.BlockSpec(memory_space=pltpu.SMEM), per_filter(per, (n, n)), per_filter(per, (n, n)), per_filter(per, (kdim, n)),
+                      whole_spec((TAPS // SUB, SUB, LANES)), whole_spec((n, n)), whole_spec((2 * hr, n)), whole_spec((2 * hr, kdim)),
+                      whole_spec((n, 2 * n)), whole_spec((n, n))],
+            out_specs=[whole_spec((tiles, SUB, LANES)), per_filter(per, (2, hr, n))],
             out_shape=[jax.ShapeDtypeStruct((tiles, SUB, LANES), f32), jax.ShapeDtypeStruct((count, 2, hr, n), f32)],
-            scratch_shapes=[pltpu.VMEM((2, n, n), bf16)] + [pltpu.VMEM((2 * hr, n), f32)] * 3,
+            scratch_shapes=[pltpu.VMEM((per, 2, n, n), bf16)] + [pltpu.VMEM((per, 2 * hr, n), f32)] * 3
+            + [pltpu.VMEM((2, hr, n), f32), pltpu.VMEM((3, 2 * hr, n), bf16), pltpu.VMEM((2 * hr, 2 * n), f32), pltpu.VMEM((2, n, n), bf16)],
             compiler_params=params,
             name="sums",
-        )(code_maps, dual_maps, td, energy, t["first"], t["second"], t["left6"])
+        )(valid_blocks, code_maps, dual_maps, td, energy, t["first"], t["second"], t["left6"], t["inv_first"], t["inv_second"])
         sums = reduce_tiles(acc, stages, lanes)
-        mask = jnp.repeat(valid_blocks, MB).astype(f32)[:, None]
+        per = filters_per_step(count, UPDATE_FILTERS)
         new_codes, new_duals, crops = pl.pallas_call(
             lambda *refs: update_kernel(n, *refs),
-            grid=(count,),
-            in_specs=[whole_spec((tiles, SUB, LANES)), whole_spec((hr, TAPS)), whole_spec((LANES, n)), whole_spec((n, n)), whole_spec((n, 1)), per_filter((2, hr, n)),
-                      per_filter((n, n)), per_filter((kdim, n)), whole_spec((n, n)), whole_spec((2 * hr, n)),
+            grid=(count // per,),
+            in_specs=[pl.BlockSpec(memory_space=pltpu.SMEM), whole_spec((tiles, SUB, LANES)), whole_spec((hr, TAPS)), whole_spec((LANES, n)), whole_spec((n, n)), per_filter(per, (2, hr, n)),
+                      per_filter(per, (n, n)), per_filter(per, (kdim, n)), whole_spec((n, n)), whole_spec((2 * hr, n)),
                       whole_spec((n, 2 * n)), whole_spec((n, n)), whole_spec((2 * hr, kdim)),
                       whole_spec((n, 128)), whole_spec((4 * PAD, 2 * hr))],
-            out_specs=[per_filter((n, n)), per_filter((n, n)), per_filter((4 * PAD, 128))],
+            out_specs=[per_filter(per, (n, n)), per_filter(per, (n, n)), per_filter(per, (4 * PAD, 128))],
             out_shape=[jax.ShapeDtypeStruct((count, n, n), bf16), jax.ShapeDtypeStruct((count, n, n), bf16),
                        jax.ShapeDtypeStruct((count, 4 * PAD, 128), f32)],
-            scratch_shapes=[pltpu.VMEM((2, hr, n), f32), pltpu.VMEM((2, hr, n), f32), pltpu.VMEM((2 * hr, n), f32),
-                            pltpu.VMEM((2 * hr, n), bf16), pltpu.VMEM((4 * hr, n), bf16),
-                            pltpu.VMEM((2 * hr, 2 * n), f32), pltpu.VMEM((n, n), bf16)],
+            scratch_shapes=[pltpu.VMEM((2, hr, n), f32), pltpu.VMEM((2, hr, n), f32), pltpu.VMEM((per, 2 * hr, n), f32),
+                            pltpu.VMEM((per, 2 * hr, n), bf16), pltpu.VMEM((per, 4 * hr, n), bf16),
+                            pltpu.VMEM((per, 2 * hr, 2 * n), f32), pltpu.VMEM((per, n, n), bf16)],
             compiler_params=params,
             name="update",
-        )(sums, t["up_rows"], t["up_cols"], survey_tile, mask, b, dual_maps, td, t["first"], t["second"], t["inv_first"],
+        )(valid_blocks, sums, t["up_rows"], t["up_cols"], survey_tile, b, dual_maps, td, t["first"], t["second"], t["inv_first"],
           t["inv_second"], t["left6"], t["crop"], t["crop_rows"])
         m = crops[:, : 2 * PAD] + crops[:, 2 * PAD :]
         m = m[:, :, : 2 * PAD] + m[:, :, 2 * PAD : 4 * PAD]

time: 96.3 us -> 88 us (0.914)
  Pallas kernels: 86.1 us -> 78.6 us
    pallas_call x1, Pallas kernels: 38.5 us -> 33.1 us  [reduce_tiles(): pl.pallas_call(lambda *refs: exchange_kernel(stages, lanes, *refs), out_s...]
    pallas_call x2, Pallas kernels: 47.5 us -> 45.6 us  [the longest x1 25.1 us: body(): pl.pallas_call(lambda *refs: update_kernel(n, *refs), grid=(count // per,...]
where the time goes in v2:
time: 88 us; the launch traced here: 87.7 us
  Pallas kernels  78.6 us (89%)
  matrix products  3.35 us (4%)
  local copies, waits for them, and re-layouts  3.3 us (4%)
  other arithmetic  1.7 us (2%)
    pallas_call x1, Pallas kernels, reduce_tiles(): pl.pallas_call(lambda *refs: exchange_kernel(stages, lanes, *refs), out_s...  33.1 us
    pallas_call x1, Pallas kernels, body(): pl.pallas_call(lambda *refs: update_kernel(n, *refs), grid=(count // per,...  25.1 us
    pallas_call x1, Pallas kernels, body(): pl.pallas_call(lambda *refs: sums_kernel(n, *refs), grid=(count // per,),...  20.5 us
    dot_general x1, matrix products, energy_samples(): jnp.dot(filters, sample, precision=lax.Precision.HIGHEST, preferred_eleme...  1.95 us

profile of v2, /device:TPU:0, one launch (start us, length us, event | category | flops | bytes accessed | tf_op | source)
XLA Modules:
  0.0 87.7 jit_solution(6524972642436570685)
XLA Ops:
  0.6 1.9 %fusion = f32[2048]{0:T(1024)S(1)} fusion(f32[121,2048]{1,0:T(8,128)} %constant.35.clone, f32[8,121]{1,0:T(8,128)} %param.19), kind=kOutput, calls=%fused_computation.2 | convolution fusion | flops 23820288 | bytes 1003296 | tf_op jit(solution)/shard_map/dot_general | solution.py:460
  2.6 0.1 reshape.27
  2.7 0.6 pad_bitcast_fusion.refs_4_
  3.3 0.8 reshape.26
  4.0 1.4 %convolution_bitcast_fusion = f32[8,11,1024]{2,1,0:T(8,128)S(1)} fusion(f32[11,1024,1]{1,0,2:T(8,128)} %constant.54, f32[8,11,11]{2,1,0:T(8,128)S(1)} %reshape.26), kind=kOutput, calls=%fused_computation.1 | convolution fusion | flops 11894784 | bytes 409376 | tf_op jit(solution)/shard_map/kab,bg->kag/dot_general | solution.py:449
  5.5 0.1 fusion.3
  5.7 0.1 fusion.2
  5.7 0.1 fusion.4
  5.8 0.0 copy-start
  5.8 1.1 %copy-done = bf16[8,192,512]{2,1,0:T(8,128)(2,1)} copy-done((bf16[8,192,512]{2,1,0:T(8,128)(2,1)}, bf16[8,192,512]{2,1,0:T(8,128)(2,1)S(1)}, u32[]{:S(2)}) %copy-start) | copy-done | bytes 1572888
  7.0 20.5 %sums.1 = (f32[416,8,128]{2,1,0:T(8,128)}, f32[8,2,272,512]{3,2,1,0:T(8,128)}) custom-call(s32[4]{0:T(128)} %refs_0_.3, bf16[8,512,512]{2,1,0:T(8,128)(2,1)} %refs_1_.1, bf16[8,512,512]{2,1,0:T(8,128)(2,1)} %refs_6_.2, bf16[8,192,512]{2,1,0:T(8,128)(2,1)} %copy-done, f32[4,8,128]{2,1,0:T(8,128)} %pad_bitcast_fusion.refs_4_, ...), custom_call_target="tpu_custom_call" | custom-call | tf_op jit(solution)/shard_map/sums/pallas_call | solution.py:518
  27.4 33.1 %exchange.1.refs_1_ = f32[416,8,128]{2,1,0:T(8,128)} custom-call(f32[416,8,128]{2,1,0:T(8,128)} %get-tuple-element.8.refs_0_), custom_call_target="tpu_custom_call" | custom-call | tf_op jit(solution)/shard_map/exchange/pallas_call | solution.py:494
  60.5 25.1 %update.1 = (bf16[8,512,512]{2,1,0:T(8,128)(2,1)}, bf16[8,512,512]{2,1,0:T(8,128)(2,1)}, f32[8,64,128]{2,1,0:T(8,128)}) custom-call(s32[4]{0:T(128)} %refs_0_.3, f32[416,8,128]{2,1,0:T(8,128)} %exchange.1.refs_1_, f32[272,32]{1,0:T(8,128)} %constant.41.clone.refs_2_, f32[128,512]{1,0:T(8,128)} %constant.42.clone.refs_3_, f32[512,512]{1,0:T(8,128)} %refs_4_.1, ...), custom_call_target="tpu_custom_call" | custom-call | tf_op jit(solution)/shard_map/update/pallas_call | solution.py:533
  85.6 1.0 %slice_add_fusion.1 = f32[8,32,128]{2,1,0:T(8,128)S(1)} fusion(f32[8,64,128]{2,1,0:T(8,128)} %get-tuple-element.12), kind=kLoop, calls=%fused_computation.16 | loop fusion | flops 32768 | bytes 393216 | tf_op jit(solution)/shard_map/add | solution.py:550
  86.6 0.1 slice_add_fusion
  86.7 0.2 multiply_reduce_fusion
  86.9 0.1 broadcast_multiply_fusion
  87.1 0.7 reshape.29
  (6 shorter events, 0.2 us)
Async XLA Ops:
  5.8 1.1 %copy-start = (bf16[8,192,512]{2,1,0:T(8,128)(2,1)}, bf16[8,192,512]{2,1,0:T(8,128)(2,1)S(1)}, u32[]{:S(2)}) copy-start(bf16[8,192,512]{2,1,0:T(8,128)(2,1)S(1)} %convert_dynamic-update-slice_fusion.2.refs_3_.refs_7_) | copy-start | bytes 4718596
